TPU v7x, 256 devices: a whole 4x4x8 slice. The times are simulated.
256 devices in a mesh: rep: 64 (over y_lo, z, x), tp: 4 (over y_hi, core).
Axes of the slice: x: 4, y: 4 (y_hi: 2, y_lo: 2; y = y_hi * 2 + y_lo), z: 8, core: 2. Of those that a mesh axis runs over, the one named last changes fastest.
Arguments:
- hidden_in: bfloat16 [64, 512, 8192], P('rep', 'tp'), may hold values from -6 to 6
- queries: bfloat16 [64, 512, 4096], P('rep', None, 'tp'), may hold values from -110 to 110
- out_grad: bfloat16 [64, 512, 4096], P('rep', None, 'tp'), may hold values from -6 to 6
- token_ids: int32 [64, 512], P('rep'), may hold values from 0 to 128000, as said below
- key_weight: bfloat16 [64, 8192, 512], P('rep', None, 'tp'), may hold values from -6 to 6
- value_weight: bfloat16 [64, 8192, 512], P('rep', None, 'tp'), may hold values from -6 to 6
- push_weight: bfloat16 [64], P('rep'), may hold values from 0.5 to 2
- gossip: int32 [16], replicated, may hold values from 0 to 2
Outputs:
- new_key_weight: bfloat16 [64, 8192, 512], P('rep', None, 'tp')
- new_value_weight: bfloat16 [64, 8192, 512], P('rep', None, 'tp')
- new_push_weight: bfloat16 [64], P('rep')
Inputs may be any that keep to these rules, and one draw needn't show every extreme that they name: `token_ids`: each replica's sequence begins with the id 128000, which marks the start of a document, and holds it at further positions now and then.
All inputs are finite; a program needn't handle non-finite values.
Results may differ from a plain program's by a relative error of at most 0.015.
The roundings to bfloat16 on the way count: a program that leaves them out, or rounds other values in their place, can miss the bound.
Values may be sent and summed in bfloat16 or wider, within the bound.
A program may use at most 128 MiB of HBM per device.

v0:
```python
from functools import partial
import math

import jax
import jax.numpy as jnp
from jax import lax
from jax.sharding import PartitionSpec as P

D = 8192
HS = 128
KVH = 4
GROUP = 8
LEVELS = 3


doc_start = 128000
learn_rate = 0.5
epsilon = 1e-06


def passed_along(x, axis, by):
    count = lax.axis_size(axis)
    return lax.ppermute(x, axis, [(i, (i + by) % count) for i in range(count)])


def by_distance(gossip, sender):
    branches = [partial(sender, 1 << exponent) for exponent in range(LEVELS)]
    return lax.switch(gossip[0], branches)


def body(hidden_in, queries, out_grad, token_ids, key_weight, value_weight, push_weight, gossip):
    width = key_weight.shape[2]
    seq_len = token_ids.shape[1]
    kv_local = width // HS
    scale_model = 1.0 / math.sqrt(D)
    head_scale = 1.0 / math.sqrt(HS)
    inverse = 1.0 / push_weight.astype(jnp.float32)[0]
    joined_weight = (
        jnp.concatenate([key_weight[0], value_weight[0]], axis=1).astype(jnp.float32) * inverse
    ).astype(jnp.bfloat16)
    gathered = lax.all_gather(hidden_in, "tp", axis=1, tiled=True)[0]
    projected = jnp.dot(gathered, joined_weight, preferred_element_type=jnp.float32) * scale_model
    key_rows = projected[:, :width].astype(jnp.bfloat16).reshape(seq_len, kv_local, HS)
    value_rows = projected[:, width:].astype(jnp.bfloat16).reshape(seq_len, kv_local, HS)
    query_heads = queries[0].reshape(seq_len, kv_local, GROUP, HS)
    segment = jnp.cumsum((token_ids[0] == doc_start).astype(jnp.int32))
    position = jnp.arange(seq_len)
    allowed = (position[None, :] <= position[:, None]) & (segment[None, :] == segment[:, None])
    scores = (
        jnp.einsum("sngd,tnd->ngst", query_heads, key_rows, preferred_element_type=jnp.float32)
        * head_scale
    )
    scores = jnp.where(allowed[None, None], scores, -1e30)
    top_score = jnp.max(scores, axis=-1, keepdims=True)
    expo = jnp.exp(scores - top_score)
    prob = expo / jnp.sum(expo, axis=-1, keepdims=True)
    prob_bf = prob.astype(jnp.bfloat16)
    outputs = jnp.einsum("ngst,tnd->sngd", prob_bf, value_rows, preferred_element_type=jnp.float32)
    grad_out = out_grad[0].reshape(seq_len, kv_local, GROUP, HS)
    delta = jnp.sum(grad_out.astype(jnp.float32) * outputs, axis=-1)
    grad_p = jnp.einsum("sngd,tnd->ngst", grad_out, value_rows, preferred_element_type=jnp.float32)
    grad_s = (prob * (grad_p - jnp.transpose(delta, (1, 2, 0))[..., None])).astype(jnp.bfloat16)
    grad_v = jnp.einsum(
        "ngst,sngd->tnd", prob_bf, grad_out, preferred_element_type=jnp.float32
    ).astype(jnp.bfloat16)
    grad_k = (
        jnp.einsum("ngst,sngd->tnd", grad_s, query_heads, preferred_element_type=jnp.float32)
        * head_scale
    ).astype(jnp.bfloat16)
    grad_pair = jnp.concatenate(
        [grad_k.reshape(seq_len, width), grad_v.reshape(seq_len, width)], axis=1
    )
    grad_weight = (
        jnp.einsum("sd,se->de", gathered, grad_pair, preferred_element_type=jnp.float32)
        * scale_model
    )
    squares = lax.psum(jnp.sum(grad_weight * grad_weight), "tp")
    factor = lax.rsqrt(squares / (2 * D * KVH * HS) + epsilon)
    direction = (grad_weight * factor).astype(jnp.bfloat16)
    dir_k = direction[:, :width][None]
    dir_v = direction[:, width:][None]

    def send_whole(distance):
        return passed_along((key_weight, value_weight, push_weight, dir_k, dir_v), "rep", distance)

    peer_key, peer_value, peer_push, peer_dir_k, peer_dir_v = by_distance(gossip, send_whole)

    def mixed(numer, peer_numer, step, peer_step):
        own = numer.astype(jnp.float32)
        return (
            0.5 * (own + peer_numer.astype(jnp.float32))
            - 0.5 * learn_rate * (step.astype(jnp.float32) + peer_step.astype(jnp.float32))
        ).astype(jnp.bfloat16)

    new_key = mixed(key_weight, peer_key, dir_k, peer_dir_k)
    new_value = mixed(value_weight, peer_value, dir_v, peer_dir_v)
    new_push = (0.5 * (push_weight.astype(jnp.float32) + peer_push.astype(jnp.float32))).astype(
        jnp.bfloat16
    )
    return (new_key, new_value, new_push)


def solution(mesh):
    return jax.shard_map(
        body,
        mesh=mesh,
        in_specs=(
            P("rep", "tp", None),
            P("rep", None, "tp"),
            P("rep", None, "tp"),
            P("rep", None),
            P("rep", None, "tp"),
            P("rep", None, "tp"),
            P("rep"),
            P(),
        ),
        out_specs=(P("rep", None, "tp"), P("rep", None, "tp"), P("rep")),
        check_vma=False,
    )
```

profile of v0, /device:TPU:2, one launch (start us, length us, event | category | flops | bytes accessed | tf_op | source)
XLA Modules:
  0.0 368.1 jit_solution(5010611359448544300)
XLA Ops:
  7.2 0.0 all-gather.2.cloned.1.call-start
  7.2 0.7 all-gather.2.cloned.1.call-update
  7.9 0.7 compare_convert_fusion
  8.6 0.3 reduce-window.9
  8.9 0.1 slice.25
  9.7 1.5 copy.68
  11.2 1.6 copy.36
  12.8 0.3 copy.69
  13.1 0.0 copy-start.4
  13.1 4.1 %copy.31 = bf16[1,8192,128]{1,2,0:T(8,128)(2,1)} copy(bf16[1,8192,128]{2,1,0:T(8,128)(2,1)} %param.15) | data formatting | bytes 4194304 | tf_op args[4]
  17.2 4.1 %copy.46 = bf16[1,8192,128]{1,2,0:T(8,128)(2,1)} copy(bf16[1,8192,128]{2,1,0:T(8,128)(2,1)} %param.16) | data formatting | bytes 4194304 | tf_op args[5]
  21.3 0.1 slice_reduce_fusion
  21.5 0.1 add_bitcast_fusion
  21.5 0.2 fusion.53
  21.8 56.0 %all-gather.2.cloned.1.call-done = bf16[1,512,8192]{2,1,0:T(8,128)(2,1)} async-done(((bf16[1,128,8192]{2,1,0:T(8,128)(2,1)}), bf16[1,512,8192]{2,1,0:T(8,128)(2,1)}) %all-gather.2.cloned.1.call-update) | async-done | bytes 8388624 | tf_op jit(solution)/shard_map/all_gather | solution.py:41
  77.7 7.0 %fusion.38 = bf16[512,256]{0,1:T(8,128)(2,1)S(1)} fusion(bf16[1,512,8192]{2,1,0:T(8,128)(2,1)} %all-gather.2.cloned.1.call-done, bf16[8192,128]{1,0:T(8,128)(2,1)} %bitcast.141, bf16[8192,128]{1,0:T(8,128)(2,1)} %bitcast.140, f32[]{:T(128)} %bitcast.5), kind=kOutput, calls=%fused_computation.38 | convolution fusion | flops 2160328704 | bytes 12845060 | tf_op jit(solution)/shard_map/dot_general | solution.py:42
  84.8 1.8 fusion.8
  86.6 0.0 copy-start.3
  86.6 1.8 fusion.7
  88.4 1.4 copy-done.3
  89.7 13.6 %fusion.26 = f32[512,8]{0,1:T(8,128)S(1)} fusion(f32[512,1,8,128]{0,3,2,1:T(8,128)S(1)} %bitcast.139, bf16[512,256]{0,1:T(8,128)(2,1)S(1)} %fusion.38, f32[8,512]{1,0:T(8,128)S(1)} %fusion.7, f32[8,512]{1,0:T(8,128)S(1)} %get-tuple-element.137, f32[512,512,8]{1,0,2:T(8,128)S(1)} %get-tuple-element.138, pred[512,512]{0,1:T(8,128)(4,1)S(1)} %fusion.53), kind=kOutput, calls=%fused_computation.34 | convolution fusion | flops 548401152 | bytes 10928128 | tf_op jit(solution)/shard_map/ngst,tnd->sngd/dot_general | solution.py:58
  103.4 2.3 fusion.47
  105.7 6.5 %fusion.50 = bf16[512,128]{1,0:T(8,128)(2,1)S(1)} fusion(f32[8,512]{1,0:T(8,128)S(1)} %bitcast.147, f32[8,512]{1,0:T(8,128)S(1)} %fusion.7, f32[8,512]{1,0:T(8,128)S(1)} %get-tuple-element.137, f32[512,512,8]{1,0,2:T(8,128)} %copy-done.1, pred[512,512]{0,1:T(8,128)(4,1)S(1)} %fusion.53, bf16[512,8,128]{2,1,0:T(8,128)(2,1)S(1)} %bitcast.144, ...), kind=kOutput, calls=%fused_computation.42 | convolution fusion | flops 1088552960 | bytes 11059200 | tf_op jit(solution)/shard_map/ngst,sngd->tnd/dot_general | solution.py:67
  112.2 9.6 %multiply_reduce_fusion = (f32[]{:T(128)}, f32[256,8192]{1,0:T(8,128)}) fusion(bf16[1,512,8192]{2,1,0:T(8,128)(2,1)} %all-gather.2.cloned.1.call-done, bf16[512,128]{1,0:T(8,128)(2,1)S(1)} %fusion.47, bf16[512,128]{1,0:T(8,128)(2,1)S(1)} %fusion.50), kind=kOutput, calls=%fused_computation.9 | convolution fusion | flops 2154299392 | bytes 17039364 | tf_op jit(solution)/shard_map/sd,se->de/dot_general | solution.py:74
  121.9 8.1 %psum.7 = f32[]{:T(128)} all-reduce(f32[]{:T(128)} %get-tuple-element.139), channel_id=1, replica_groups=mesh['rep'=64,'tp'=4] {'tp'}, use_global_device_ids=true, to_apply=%region_6.7 | all-reduce | flops 1 | bytes 8 | tf_op jit(solution)/shard_map/psum | solution.py:77
  130.7 4.0 %fusion.9 = bf16[8192,256]{0,1:T(8,128)(2,1)S(1)} fusion(f32[256,8192]{1,0:T(8,128)} %get-tuple-element.140, f32[]{:T(128)S(6)} %mul.93), kind=kLoop, calls=%fused_computation.15 | loop fusion | flops 4194304 | bytes 12582916 | tf_op jit(solution)/shard_map/convert_element_type | solution.py:79
  134.8 1.9 slice_bitcast_fusion
  136.7 0.7 copy-done
  137.4 205.3 %conditional.3 = (f32[1]{0:T(128)}, f32[1,8192,128]{1,2,0:T(8,128)}, f32[1,8192,128]{1,2,0:T(8,128)}, f32[1,8192,128]{1,2,0:T(8,128)}, f32[1,8192,128]{1,2,0:T(8,128)}) conditional(s32[]{:T(128)} %bitcast, (bf16[1,8192,128]{2,1,0:T(8,128)(2,1)}, bf16[1,8192,128]{2,1,0:T(8,128)(2,1)}, bf16[1]{0:T(256)(128)(2,1)}, ...), branch_computations={%region_7.8_spmd, %region_8.9_spmd, %region_9.10_spmd} | conditional | flops 1 | bytes 67109120
  137.4 4.1 %copy.42 = bf16[1,8192,128]{2,1,0:T(8,128)(2,1)} copy(bf16[1,8192,128]{1,2,0:T(8,128)(2,1)} %get-tuple-element.124) | data formatting | bytes 4194304 | tf_op jit(solution)/shard_map
  141.5 1.6 collective-permute-start.13
  143.0 2.4 copy.43
  145.5 1.6 collective-permute-start.14
  147.0 1.6 collective-permute-start.10
  148.6 2.8 collective-permute-start.11
  151.4 0.6 collective-permute-start.12
  152.0 173.6 %collective-permute-done.12 = bf16[1]{0:T(256)(128)(2,1)} collective-permute-done((bf16[1]{0:T(256)(128)(2,1)}, bf16[1]{0:T(256)(128)(2,1)}, u32[]{:S(2)}, u32[]{:S(2)}) %collective-permute-start.12) | collective-permute-done | bytes 34 | tf_op jit(solution)/shard_map/cond/branch_2_fun/ppermute | solution.py:23
  326.3 0.0 collective-permute-done.13
  326.3 4.3 %copy.61 = f32[1,8192,128]{1,2,0:T(8,128)} copy(bf16[1,8192,128]{2,1,0:T(8,128)(2,1)} %collective-permute-done.13) | data formatting | bytes 6291456 | tf_op jit(solution)/shard_map/conditional.1
  330.6 0.0 collective-permute-done.14
  330.6 4.3 %copy.67 = f32[1,8192,128]{1,2,0:T(8,128)} copy(bf16[1,8192,128]{2,1,0:T(8,128)(2,1)} %collective-permute-done.14) | data formatting | bytes 6291456 | tf_op jit(solution)/shard_map/conditional.1
  334.9 0.0 collective-permute-done.10
  334.9 4.3 %copy.58 = f32[1,8192,128]{1,2,0:T(8,128)} copy(bf16[1,8192,128]{2,1,0:T(8,128)(2,1)} %collective-permute-done.10) | data formatting | bytes 6291456 | tf_op jit(solution)/shard_map/conditional.1
  339.3 0.0 collective-permute-done.11
  339.3 3.4 copy.64
  342.7 10.6 %subtract_convert_fusion = (bf16[1,8192,128]{1,2,0:T(8,128)(2,1)S(1)}, bf16[1,8192,128]{1,2,0:T(8,128)(2,1)}) fusion(f32[1,8192,128]{1,2,0:T(8,128)} %get-tuple-element.132, f32[1,8192,128]{1,2,0:T(8,128)} %get-tuple-element.131, bf16[1,8192,128]{1,2,0:T(8,128)(2,1)} %copy.46, bf16[8192,256]{0,1:T(8,128)(2,1)} %copy-done, ...), kind=kLoop, calls=%fused_computation.25 | loop fusion | flops 16777216 | bytes 29360128 | tf_op jit(solution)/shard_map/convert_element_type | solution.py:93
  353.3 4.1 %copy.49 = bf16[1,8192,128]{2,1,0:T(8,128)(2,1)} copy(bf16[1,8192,128]{1,2,0:T(8,128)(2,1)} %get-tuple-element.134) | data formatting | bytes 4194304
  357.4 2.4 copy.50
  (7 shorter events, 0.0 us)
Async XLA Ops:
  7.2 4.0 %copy-start.2 = (bf16[1,512,1024]{2,1,0:T(8,128)(2,1)S(1)}, bf16[1,512,1024]{2,1,0:T(8,128)(2,1)}, u32[]{:S(2)}) copy-start(bf16[1,512,1024]{2,1,0:T(8,128)(2,1)} %param.13) | copy-start | bytes 3145732
  7.2 70.5 %all-gather.2.cloned.1.call-start = ((), (), s32[]{:S(2)}) async-start(), calls=%async_computation | async-start | bytes 10485760 | tf_op jit(solution)/shard_map/all_gather | solution.py:41
  13.1 8.2 %copy-start.4 = (s32[16]{0:T(128)S(1)}, s32[16]{0:T(128)}, u32[]{:S(2)}) copy-start(s32[16]{0:T(128)} %param.18) | copy-start | bytes 196
  86.6 16.8 %copy-start.1 = (f32[512,512,8]{1,0,2:T(8,128)}, f32[512,512,8]{1,0,2:T(8,128)S(1)}, u32[]{:S(2)}) copy-start(f32[512,512,8]{1,0,2:T(8,128)S(1)} %get-tuple-element.138) | copy-start | bytes 25165828
  86.6 3.2 copy-start.3
  134.8 2.6 copy-start
  141.5 184.8 %collective-permute-start.13 = (bf16[1,8192,128]{2,1,0:T(8,128)(2,1)}, bf16[1,8192,128]{2,1,0:T(8,128)(2,1)}, u32[]{:S(2)}, u32[]{:S(2)}) collective-permute-start(bf16[1,8192,128]{2,1,0:T(8,128)(2,1)} %copy.42), channel_id=1, source_target_pairs={{0,16},{4,20},{8,24},{12,28},{16,32},{20,36},{24,40},{28,44},{32,4... | collective-permute-start | bytes 6291464 | tf_op jit(solution)/shard_map/cond/branch_2_fun/ppermute | solution.py:23
  145.5 185.1 %collective-permute-start.14 = (bf16[1,8192,128]{2,1,0:T(8,128)(2,1)}, bf16[1,8192,128]{2,1,0:T(8,128)(2,1)}, u32[]{:S(2)}, u32[]{:S(2)}) collective-permute-start(bf16[1,8192,128]{2,1,0:T(8,128)(2,1)} %copy.43), channel_id=1, source_target_pairs={{0,16},{4,20},{8,24},{12,28},{16,32},{20,36},{24,40},{28,44},{32,4... | collective-permute-start | bytes 6291464 | tf_op jit(solution)/shard_map/cond/branch_2_fun/ppermute | solution.py:23
  147.0 187.9 %collective-permute-start.10 = (bf16[1,8192,128]{2,1,0:T(8,128)(2,1)}, bf16[1,8192,128]{2,1,0:T(8,128)(2,1)}, u32[]{:S(2)}, u32[]{:S(2)}) collective-permute-start(bf16[1,8192,128]{2,1,0:T(8,128)(2,1)} %get-tuple-element.70), channel_id=1, source_target_pairs={{0,16},{4,20},{8,24},{12,28},{16,32},{20,36},{24,40},{28,44},{32,4... | collective-permute-start | bytes 6291464 | tf_op jit(solution)/shard_map/cond/branch_2_fun/ppermute | solution.py:23
  148.6 190.7 %collective-permute-start.11 = (bf16[1,8192,128]{2,1,0:T(8,128)(2,1)}, bf16[1,8192,128]{2,1,0:T(8,128)(2,1)S(1)}, u32[]{:S(2)}, u32[]{:S(2)}) collective-permute-start(bf16[1,8192,128]{2,1,0:T(8,128)(2,1)} %get-tuple-element.71), channel_id=1, source_target_pairs={{0,16},{4,20},{8,24},{12,28},{16,32},{20,36},{24,40},{28,44},{32,4... | collective-permute-start | bytes 6291464 | tf_op jit(solution)/shard_map/cond/branch_2_fun/ppermute | solution.py:23
  151.4 174.3 %collective-permute-start.12 = (bf16[1]{0:T(256)(128)(2,1)}, bf16[1]{0:T(256)(128)(2,1)}, u32[]{:S(2)}, u32[]{:S(2)}) collective-permute-start(bf16[1]{0:T(256)(128)(2,1)} %get-tuple-element.72), channel_id=1, source_target_pairs={{0,16},{4,20},{8,24},{12,28},{16,32},{20,36},{24,40},{28,44},{32,4... | collective-permute-start | bytes 14 | tf_op jit(solution)/shard_map/cond/branch_2_fun/ppermute | solution.py:23
Sparse Core Ops, SparseCore 0:
  9.8 67.8 all-gather.1
where the time goes:
time: 375 us; the launch traced here: 368 us
  waiting for transfers between devices  230 us (61%)
  local copies, waits for them, and re-layouts  45.1 us (12%)
  matrix products  41 us (11%)
  other arithmetic  17.7 us (5%)
  between operations  17.1 us (5%)
  starting transfers between devices  8.14 us (2%)
  blocking collectives  8.14 us (2%)
    ppermute x5, waiting for transfers between devices, passed_along(): return lax.ppermute(x, axis, [(i, (i + by) % count) for i in range(count)])  174 us
    all_gather x1, waiting for transfers between devices, body(): gathered = lax.all_gather(hidden_in, 'tp', axis=1, tiled=True)[0]  56 us
    another operation x7, local copies, waits for them, and re-layouts  23 us
    unnamed x16, local copies, waits for them, and re-layouts  18.5 us
    dot_general x1, matrix products, body(): jnp.einsum('ngst,tnd->sngd', prob_bf, value_rows, preferred_element_type=...  13.6 us
    convert_element_type x1, other arithmetic, mixed(): return (0.5 * (own + peer_numer.astype(jnp.float32)) - 0.5 * learn_rate *...  10.6 us
    dot_general x1, matrix products, body(): jnp.einsum('sd,se->de', gathered, grad_pair, preferred_element_type=jnp.f...  9.63 us
    psum x1, blocking collectives, body(): squares = lax.psum(jnp.sum(grad_weight * grad_weight), 'tp')  8.14 us
  transfers between devices with their start and end apart: 6, of which 2 were waited for; matrix products, arithmetic and copies ran while one was open for 8% of the time, Pallas kernels for 0%

commit v1 on v0

v1 whole, which is shorter than its diff:
```python
from functools import partial
import math

import jax
import jax.numpy as jnp
from jax import lax
from jax.experimental import pallas as pl
from jax.experimental.pallas import tpu as pltpu
from jax.sharding import PartitionSpec as P

D = 8192
HS = 128
KVH = 4
GROUP = 8
LEVELS = 3
TOK = 128
SEQ = 512
N_REP = 64

doc_start = 128000
learn_rate = 0.5
epsilon = 1e-06

MESH = pl.DeviceIdType.MESH
BF = jnp.bfloat16
F32 = jnp.float32
MIB = 1024 * 1024

COLS = 1024
N_IN = D // COLS
ROWS = 512
N_OUT = D // ROWS


def dot_nn(a, b):
    return lax.dot_general(a, b, (((1,), (0,)), ((), ())), preferred_element_type=F32)


def dot_nt(a, b):
    return lax.dot_general(a, b, (((1,), (1,)), ((), ())), preferred_element_type=F32)


def dot_tn(a, b):
    return lax.dot_general(a, b, (((0,), (0,)), ((), ())), preferred_element_type=F32)


def kernel(
    distance,
    hid, qin, gin, ids, kin, vin, push,
    out_k, out_v, out_push,
    hbuf, qbuf, gbuf, kw, vw, bias, zbuf, acc, krow, vrow, gk, gv, gpair, gw, sqacc,
    abuf, rbuf, ostk, ostv, sq_mine, sq_peer, push_mine, push_peer,
    load_sem, y2_send, y2_recv, fw_send, fw_recv, core_send, core_recv,
    sq_send, sq_recv, rep_send, rep_recv, push_send, push_recv, out_sem,
):
    rep = lax.axis_index("rep")
    tp = lax.axis_index("tp")
    half = tp // 2
    core = lax.rem(tp, 2)
    other_core = (rep, half * 2 + 1 - core)
    other_half = (rep, (1 - half) * 2 + core)
    diagonal = (rep, (1 - half) * 2 + 1 - core)
    target = (lax.rem(rep + distance, N_REP), tp)
    source = (lax.rem(rep + N_REP - distance, N_REP), tp)

    mine = pl.ds(pl.multiple_of(tp * TOK, TOK), TOK)
    theirs = pl.ds(pl.multiple_of(other_half[1] * TOK, TOK), TOK)

    def remote(src, dst, send, recv, device):
        return pltpu.make_async_remote_copy(
            src_ref=src, dst_ref=dst, send_sem=send, recv_sem=recv,
            device_id=device, device_id_type=MESH,
        )

    loads = [
        pltpu.make_async_copy(src, dst, load_sem.at[n])
        for n, (src, dst) in enumerate(
            [(kin, kw), (vin, vw), (hid, hbuf.at[mine]), (qin, qbuf), (gin, gbuf)]
        )
    ]
    for copy in loads:
        copy.start()

    barrier = pltpu.get_barrier_semaphore()
    for device in (other_core, other_half, diagonal, source):
        pl.semaphore_signal(barrier, inc=1, device_id=device, device_id_type=MESH)
    pl.semaphore_wait(barrier, 4)

    def across(i):
        cols = pl.ds(pl.multiple_of(i * COLS, COLS), COLS)
        return remote(
            hid.at[:, cols], hbuf.at[mine, cols], y2_send.at[i], y2_recv.at[i], other_half
        )

    def onward(i):
        cols = pl.ds(pl.multiple_of(i * COLS, COLS), COLS)
        return remote(
            hbuf.at[theirs, cols], hbuf.at[theirs, cols], fw_send.at[i], fw_recv.at[i], other_core
        )

    def start_across(i, carry):
        across(i).start()
        return carry

    lax.fori_loop(0, N_IN, start_across, 0)
    beside = remote(hid, hbuf.at[mine], core_send, core_recv, other_core)
    beside.start()
    push_f32 = push[0:1, 0:1].astype(F32)
    push_mine[...] = jnp.broadcast_to(push_f32, (8, 128))
    push_along = remote(push_mine, push_peer, push_send, push_recv, target)
    push_along.start()

    with jax.named_scope("mask"):
        down = lax.broadcasted_iota(jnp.int32, (SEQ, SEQ), 0)
        over = lax.broadcasted_iota(jnp.int32, (SEQ, SEQ), 1)
        starts = jnp.broadcast_to((ids[...] == doc_start).astype(F32), (8, SEQ)).astype(BF)
        upper = (down <= over).astype(F32).astype(BF)
        lower = (over <= down).astype(F32).astype(BF)
        seg_row = dot_nn(starts, upper)
        seg_col = dot_nt(lower, starts)
        allowed = (down <= over) & (seg_col[:, 0:1] == seg_row[0:1, :])
        bias[...] = jnp.where(allowed, 0.0, -1e30)

    acc[...] = jnp.zeros_like(acc)
    gk[...] = jnp.zeros_like(gk)
    gv[...] = jnp.zeros_like(gv)
    sqacc[...] = jnp.zeros_like(sqacc)
    inverse = 1.0 / push_f32
    for copy in loads:
        copy.wait()
    beside.wait()

    def project(i, carry):
        @pl.when(i < N_IN)
        def _():
            across(i).wait_recv()
            onward(i).start()

        @pl.when(i > 0)
        def _():
            j = i - 1
            onward(j).wait_recv()
            rows = pl.ds(pl.multiple_of(j * COLS, COLS), COLS)
            zbuf[:, 0:HS] = (kw[rows, :].astype(F32) * inverse).astype(BF)
            zbuf[:, HS:] = (vw[rows, :].astype(F32) * inverse).astype(BF)
            acc[...] += dot_nn(hbuf[:, rows], zbuf[...])

        return carry

    with jax.named_scope("project"):
        lax.fori_loop(0, N_IN + 1, project, 0)

    scale_model = 1.0 / math.sqrt(D)
    head_scale = 1.0 / math.sqrt(HS)
    krow[...] = (acc[:, 0:HS] * scale_model).astype(BF)
    vrow[...] = (acc[:, HS:] * scale_model).astype(BF)

    def head(g, carry):
        lanes = pl.ds(pl.multiple_of(g * HS, HS), HS)
        for first, count, keys in ((0, 256, 256), (256, 256, 512)):
            query = qbuf[first : first + count, lanes]
            grad = gbuf[first : first + count, lanes]
            scores = dot_nt(krow[0:keys, :], query) * head_scale
            scores = scores + bias[0:keys, first : first + count]
            grad_p = dot_nt(vrow[0:keys, :], grad)
            expo = jnp.exp(scores - jnp.max(scores, axis=0, keepdims=True))
            prob = expo * (1.0 / jnp.sum(expo, axis=0, keepdims=True))
            prob_bf = prob.astype(BF)
            delta = jnp.sum(prob_bf.astype(F32) * grad_p, axis=0, keepdims=True)
            grad_s = (prob * (grad_p - delta)).astype(BF)
            gv[0:keys, :] += dot_nn(prob_bf, grad)
            gk[0:keys, :] += dot_nn(grad_s, query)
        return carry

    with jax.named_scope("attend"):
        lax.fori_loop(0, GROUP, head, 0)
    gpair[:, 0:HS] = (gk[...] * head_scale).astype(BF)
    gpair[:, HS:] = gv[...].astype(BF)

    def weight_grad(i, carry):
        rows = pl.ds(pl.multiple_of(i * ROWS, ROWS), ROWS)
        g = dot_tn(hbuf[:, rows], gpair[...]) * scale_model
        gw[rows, :] = g
        sqacc[...] += jnp.sum((g * g).reshape(ROWS // 8, 8, 2 * HS), axis=0)
        return carry

    with jax.named_scope("weight_grad"):
        lax.fori_loop(0, N_OUT, weight_grad, 0)

    sq_mine[...] = jnp.broadcast_to(jnp.sum(sqacc[...], keepdims=True), (8, 128))
    shares = [
        remote(sq_mine, sq_peer.at[n], sq_send.at[n], sq_recv.at[n], device)
        for n, device in enumerate((other_core, other_half, diagonal))
    ]
    for copy in shares:
        copy.start()
    for copy in shares:
        copy.wait()
    squares = (sq_mine[0:1, 0:1] + sq_peer[0, 0:1, 0:1]) + (
        sq_peer[1, 0:1, 0:1] + sq_peer[2, 0:1, 0:1]
    )
    factor = lax.rsqrt(squares / (2 * D * KVH * HS) + epsilon)

    def own_part(rows):
        step = (gw[rows, :] * factor).astype(BF).astype(F32)
        own_k = 0.5 * kw[rows, :].astype(F32) - (0.5 * learn_rate) * step[:, 0:HS]
        own_v = 0.5 * vw[rows, :].astype(F32) - (0.5 * learn_rate) * step[:, HS:]
        return own_k, own_v

    def along(i):
        rows = pl.ds(pl.multiple_of(i * ROWS, ROWS), ROWS)
        return remote(abuf.at[rows], rbuf.at[rows], rep_send.at[i], rep_recv.at[i], target)

    def send_part(i, carry):
        rows = pl.ds(pl.multiple_of(i * ROWS, ROWS), ROWS)
        own_k, own_v = own_part(rows)
        abuf[rows, 0:HS] = own_k.astype(BF)
        abuf[rows, HS:] = own_v.astype(BF)
        along(i).start()
        return carry

    with jax.named_scope("send_parts"):
        lax.fori_loop(0, N_OUT, send_part, 0)

    push_along.wait()
    out_push[...] = (0.5 * (push_f32 + push_peer[0:1, 0:1])).astype(BF)

    def written(i):
        rows = pl.ds(pl.multiple_of(i * ROWS, ROWS), ROWS)
        return (
            pltpu.make_async_copy(ostk.at[rows], out_k.at[rows], out_sem.at[0, i]),
            pltpu.make_async_copy(ostv.at[rows], out_v.at[rows], out_sem.at[1, i]),
        )

    def mix(i, carry):
        rows = pl.ds(pl.multiple_of(i * ROWS, ROWS), ROWS)
        own_k, own_v = own_part(rows)
        along(i).wait_recv()
        ostk[rows, :] = (own_k + rbuf[rows, 0:HS].astype(F32)).astype(BF)
        ostv[rows, :] = (own_v + rbuf[rows, HS:].astype(F32)).astype(BF)
        for copy in written(i):
            copy.start()
        return carry

    with jax.named_scope("mix"):
        lax.fori_loop(0, N_OUT, mix, 0)

    def finish(i, carry):
        along(i).wait_send()
        for copy in written(i):
            copy.wait()
        return carry

    lax.fori_loop(0, N_OUT, finish, 0)

    def sent(i, carry):
        across(i).wait_send()
        onward(i).wait_send()
        return carry

    lax.fori_loop(0, N_IN, sent, 0)


def run(level, hid, qin, gin, ids, kin, vin, push):
    vmem = pltpu.VMEM
    dma = pltpu.SemaphoreType.DMA
    whole = pl.BlockSpec(memory_space=pltpu.VMEM)
    hbm = pl.BlockSpec(memory_space=pl.ANY)
    return pl.pallas_call(
        partial(kernel, 1 << level),
        name=f"gossip_step_{1 << level}",
        out_shape=(
            jax.ShapeDtypeStruct((D, HS), BF),
            jax.ShapeDtypeStruct((D, HS), BF),
            jax.ShapeDtypeStruct((1, 1), BF),
        ),
        in_specs=[hbm, hbm, hbm, whole, hbm, hbm, whole],
        out_specs=(hbm, hbm, whole),
        scratch_shapes=[
            vmem((SEQ, D), BF),
            vmem((SEQ, GROUP * HS), BF),
            vmem((SEQ, GROUP * HS), BF),
            vmem((D, HS), BF),
            vmem((D, HS), BF),
            vmem((SEQ, SEQ), F32),
            vmem((COLS, 2 * HS), BF),
            vmem((SEQ, 2 * HS), F32),
            vmem((SEQ, HS), BF),
            vmem((SEQ, HS), BF),
            vmem((SEQ, HS), F32),
            vmem((SEQ, HS), F32),
            vmem((SEQ, 2 * HS), BF),
            vmem((D, 2 * HS), F32),
            vmem((8, 2 * HS), F32),
            vmem((D, 2 * HS), BF),
            vmem((D, 2 * HS), BF),
            vmem((D, HS), BF),
            vmem((D, HS), BF),
            vmem((8, 128), F32),
            vmem((3, 8, 128), F32),
            vmem((8, 128), F32),
            vmem((8, 128), F32),
            dma((5,)),
            dma((N_IN,)),
            dma((N_IN,)),
            dma((N_IN,)),
            dma((N_IN,)),
            dma,
            dma,
            dma((3,)),
            dma((3,)),
            dma((N_OUT,)),
            dma((N_OUT,)),
            dma,
            dma,
            dma((2, N_OUT)),
        ],
        compiler_params=pltpu.CompilerParams(
            collective_id=level, has_side_effects=True, vmem_limit_bytes=58 * MIB
        ),
        cost_estimate=pl.CostEstimate(
            flops=7_000_000_000, bytes_accessed=16 * MIB, transcendentals=2_000_000
        ),
    )(hid, qin, gin, ids, kin, vin, push)


def body(hidden_in, queries, out_grad, token_ids, key_weight, value_weight, push_weight, gossip):
    args = (
        hidden_in[0], queries[0], out_grad[0], token_ids, key_weight[0], value_weight[0],
        push_weight.reshape(1, 1),
    )
    new_key, new_value, new_push = lax.switch(
        gossip[0], [partial(run, level) for level in range(LEVELS)], *args
    )
    return new_key[None], new_value[None], new_push.reshape(1)


def solution(mesh):
    return jax.shard_map(
        body,
        mesh=mesh,
        in_specs=(
            P("rep", "tp", None),
            P("rep", None, "tp"),
            P("rep", None, "tp"),
            P("rep", None),
            P("rep", None, "tp"),
            P("rep", None, "tp"),
            P("rep"),
            P(),
        ),
        out_specs=(P("rep", None, "tp"), P("rep", None, "tp"), P("rep")),
        check_vma=False,
    )
```

time: 375 us -> 178 us (0.47)
  the two profiles are of different devices: /device:TPU:2 before, /device:TPU:1 now
where the time goes in v1:
time: 178 us
  Pallas kernels  172 us (97%)
  between operations  3.04 us (2%)
  local copies, waits for them, and re-layouts  2.64 us (1%)
    pallas_call x1, Pallas kernels, run(): pl.pallas_call(partial(kernel, 1 << level), name=f'gossip_step_{1 << leve...  172 us

profile of v1, /device:TPU:1, one launch (start us, length us, event | category | flops | bytes accessed | tf_op | source)
XLA Modules:
  0.0 177.8 jit_solution(2181794945363524404)
XLA Ops:
  1.3 172.2 %conditional.1 = ((bf16[8192,128]{1,0:T(8,128)(2,1)S(1)}, bf16[8192,128]{1,0:T(8,128)(2,1)S(1)}, bf16[1,1]{1,0:T(2,128)(2,1)})) conditional(s32[]{:T(128)} %bitcast, (bf16[128,8192]{1,0:T(8,128)(2,1)}, bf16[512,1024]{1,0:T(8,128)(2,1)}, bf16[512,1024]{1,0:T(8,128)(2,1)}, s32[1,512]{1,0:T(1,128)}, bf16[8192,128]{1,0:T(8,128)(2,1)}, ...), branch_computations={%region_0.0_spmd, %region_1.0_spmd, %region_2.0_spmd} | conditional | flops 7000000000 | bytes 16777224 | solution.py:332
  1.3 172.1 %gossip_step_4.1 = (bf16[8192,128]{1,0:T(8,128)(2,1)S(1)}, bf16[8192,128]{1,0:T(8,128)(2,1)S(1)}, bf16[1,1]{1,0:T(2,128)(2,1)}) custom-call(bf16[128,8192]{1,0:T(8,128)(2,1)} %get-tuple-element.74.hid, bf16[512,1024]{1,0:T(8,128)(2,1)} %get-tuple-element.75.qin, bf16[512,1024]{1,0:T(8,128)(2,1)} %get-tuple-element.76.gin, s32[1,512]{1,0:T(1,128)} %get-tuple-element.77.ids, ...), custom_call_target="tpu_custom_call" | custom-call | flops 7000000000 | bytes 16777216 | tf_op jit(solution)/shard_map/cond/branch_2_fun/gossip_step_4/pallas_call | solution.py:269
  173.4 1.3 copy.23
  174.8 1.3 copy.24

commit v2 on v1

--- a/solution.py
+++ b/solution.py
@@ -26,10 +26,14 @@
 F32 = jnp.float32
 MIB = 1024 * 1024
 
-COLS = 1024
+COLS = 512
 N_IN = D // COLS
-ROWS = 512
+ROWS = 256
 N_OUT = D // ROWS
+BLOCK = 128
+N_BLOCK = SEQ // BLOCK
+SPAN = 1
+WIDE = 1024
 
 
 def dot_nn(a, b):
@@ -48,10 +52,12 @@
     distance,
     hid, qin, gin, ids, kin, vin, push,
     out_k, out_v, out_push,
-    hbuf, qbuf, gbuf, kw, vw, bias, zbuf, acc, krow, vrow, gk, gv, gpair, gw, sqacc,
-    abuf, rbuf, ostk, ostv, sq_mine, sq_peer, push_mine, push_peer,
+    hbuf, qbuf, gbuf, kw, vw, bias, zbuf, acc, krow, vrow, gk, gv, gpair, gw,
+    abuf, rbuf, ostk, ostv, gram,
+    sq_mine, sq_peer, push_mine, push_peer,
     load_sem, y2_send, y2_recv, fw_send, fw_recv, core_send, core_recv,
-    sq_send, sq_recv, rep_send, rep_recv, push_send, push_recv, out_sem,
+    sq_send, sq_recv, rep_send, rep_recv, push_send, push_recv,
+    credit, head_sem, out_sem,
 ):
     rep = lax.axis_index("rep")
     tp = lax.axis_index("tp")
@@ -75,8 +81,17 @@
     loads = [
         pltpu.make_async_copy(src, dst, load_sem.at[n])
         for n, (src, dst) in enumerate(
-            [(kin, kw), (vin, vw), (hid, hbuf.at[mine]), (qin, qbuf), (gin, gbuf)]
-        )
+            [(kin, kw), (vin, vw), (hid, hbuf.at[mine])]
+        )
+    ]
+    head_loads = [
+        pltpu.make_async_copy(
+            src.at[:, :, pl.ds(g * HS, HS)],
+            dst.at[:, pl.ds(g * BLOCK, BLOCK), :],
+            head_sem.at[n, g],
+        )
+        for n, (src, dst) in enumerate([(qin, qbuf), (gin, gbuf)])
+        for g in range(GROUP)
     ]
     for copy in loads:
         copy.start()
@@ -109,6 +124,8 @@
     push_mine[...] = jnp.broadcast_to(push_f32, (8, 128))
     push_along = remote(push_mine, push_peer, push_send, push_recv, target)
     push_along.start()
+    for copy in head_loads:
+        copy.start()
 
     with jax.named_scope("mask"):
         down = lax.broadcasted_iota(jnp.int32, (SEQ, SEQ), 0)
@@ -124,7 +141,7 @@
     acc[...] = jnp.zeros_like(acc)
     gk[...] = jnp.zeros_like(gk)
     gv[...] = jnp.zeros_like(gv)
-    sqacc[...] = jnp.zeros_like(sqacc)
+    gram[...] = jnp.zeros_like(gram)
     inverse = 1.0 / push_f32
     for copy in loads:
         copy.wait()
@@ -143,7 +160,9 @@
             rows = pl.ds(pl.multiple_of(j * COLS, COLS), COLS)
             zbuf[:, 0:HS] = (kw[rows, :].astype(F32) * inverse).astype(BF)
             zbuf[:, HS:] = (vw[rows, :].astype(F32) * inverse).astype(BF)
-            acc[...] += dot_nn(hbuf[:, rows], zbuf[...])
+            part = hbuf[:, rows]
+            acc[...] += dot_nn(part, zbuf[...])
+            gram[...] += dot_nt(part, part)
 
         return carry
 
@@ -155,51 +174,71 @@
     krow[...] = (acc[:, 0:HS] * scale_model).astype(BF)
     vrow[...] = (acc[:, HS:] * scale_model).astype(BF)
 
-    def head(g, carry):
-        lanes = pl.ds(pl.multiple_of(g * HS, HS), HS)
-        for first, count, keys in ((0, 256, 256), (256, 256, 512)):
-            query = qbuf[first : first + count, lanes]
-            grad = gbuf[first : first + count, lanes]
-            scores = dot_nt(krow[0:keys, :], query) * head_scale
-            scores = scores + bias[0:keys, first : first + count]
-            grad_p = dot_nt(vrow[0:keys, :], grad)
-            expo = jnp.exp(scores - jnp.max(scores, axis=0, keepdims=True))
-            prob = expo * (1.0 / jnp.sum(expo, axis=0, keepdims=True))
-            prob_bf = prob.astype(BF)
-            delta = jnp.sum(prob_bf.astype(F32) * grad_p, axis=0, keepdims=True)
-            grad_s = (prob * (grad_p - delta)).astype(BF)
-            gv[0:keys, :] += dot_nn(prob_bf, grad)
-            gk[0:keys, :] += dot_nn(grad_s, query)
+    for copy in head_loads:
+        copy.wait()
+
+    def attend(keys, query, grad, mask):
+        scores = dot_nt(krow[0:keys, :], query) * (head_scale * math.log2(math.e))
+        scores = scores + jnp.concatenate([mask] * (query.shape[0] // BLOCK), axis=1)
+        expo = jnp.exp2(scores - jnp.max(scores, axis=0, keepdims=True))
+        grad_p = dot_nt(vrow[0:keys, :], grad)
+        prob = expo * (1.0 / jnp.sum(expo, axis=0, keepdims=True))
+        prob_bf = prob.astype(BF)
+        delta = jnp.sum(prob_bf.astype(F32) * grad_p, axis=0, keepdims=True)
+        grad_s = (prob * (grad_p - delta)).astype(BF)
+        gv[0:keys, :] += dot_nn(prob_bf, grad)
+        gk[0:keys, :] += dot_nn(grad_s, query)
+
+    def attend_step(first, keys, n, carry):
+        per_block = GROUP * BLOCK // WIDE
+        block = first + n // per_block
+        rows = pl.ds(pl.multiple_of(lax.rem(n, per_block) * WIDE, WIDE), WIDE)
+        lanes = pl.ds(pl.multiple_of(block * BLOCK, BLOCK), BLOCK)
+        attend(keys, qbuf[block, rows, :], gbuf[block, rows, :], bias[0:keys, lanes])
         return carry
 
     with jax.named_scope("attend"):
-        lax.fori_loop(0, GROUP, head, 0)
+        for first in range(0, N_BLOCK, SPAN):
+            lax.fori_loop(
+                0,
+                SPAN * GROUP * BLOCK // WIDE,
+                partial(attend_step, first, (first + SPAN) * BLOCK),
+                0,
+            )
     gpair[:, 0:HS] = (gk[...] * head_scale).astype(BF)
     gpair[:, HS:] = gv[...].astype(BF)
 
-    def weight_grad(i, carry):
-        rows = pl.ds(pl.multiple_of(i * ROWS, ROWS), ROWS)
-        g = dot_tn(hbuf[:, rows], gpair[...]) * scale_model
-        gw[rows, :] = g
-        sqacc[...] += jnp.sum((g * g).reshape(ROWS // 8, 8, 2 * HS), axis=0)
-        return carry
-
-    with jax.named_scope("weight_grad"):
-        lax.fori_loop(0, N_OUT, weight_grad, 0)
-
-    sq_mine[...] = jnp.broadcast_to(jnp.sum(sqacc[...], keepdims=True), (8, 128))
+    with jax.named_scope("squares"):
+        pair = gpair[...]
+        high = gram[...].astype(BF)
+        rest = gram[...] - high.astype(F32)
+        middle = rest.astype(BF)
+        low = (rest - middle.astype(F32)).astype(BF)
+        spread = dot_nn(low, pair) + dot_nn(middle, pair) + dot_nn(high, pair)
+        total = jnp.sum(spread * pair.astype(F32), keepdims=True)
+        sq_mine[...] = jnp.broadcast_to(
+            jnp.maximum(total, 0.0) * (scale_model * scale_model), (8, 128)
+        )
     shares = [
         remote(sq_mine, sq_peer.at[n], sq_send.at[n], sq_recv.at[n], device)
         for n, device in enumerate((other_core, other_half, diagonal))
     ]
     for copy in shares:
         copy.start()
+
+    def weight_grad(i):
+        rows = pl.ds(pl.multiple_of(i * ROWS, ROWS), ROWS)
+        gw[rows, :] = dot_tn(hbuf[:, rows], gpair[...]) * scale_model
+
+    weight_grad(0)
+    push_along.wait()
     for copy in shares:
         copy.wait()
     squares = (sq_mine[0:1, 0:1] + sq_peer[0, 0:1, 0:1]) + (
         sq_peer[1, 0:1, 0:1] + sq_peer[2, 0:1, 0:1]
     )
     factor = lax.rsqrt(squares / (2 * D * KVH * HS) + epsilon)
+    pl.semaphore_signal(credit, inc=1, device_id=source, device_id_type=MESH)
 
     def own_part(rows):
         step = (gw[rows, :] * factor).astype(BF).astype(F32)
@@ -216,13 +255,22 @@
         own_k, own_v = own_part(rows)
         abuf[rows, 0:HS] = own_k.astype(BF)
         abuf[rows, HS:] = own_v.astype(BF)
+
+        @pl.when(i == 0)
+        def _():
+            pl.semaphore_wait(credit, 1)
+
         along(i).start()
+
+        @pl.when(i + 1 < N_OUT)
+        def _():
+            weight_grad(i + 1)
+
         return carry
 
     with jax.named_scope("send_parts"):
         lax.fori_loop(0, N_OUT, send_part, 0)
 
-    push_along.wait()
     out_push[...] = (0.5 * (push_f32 + push_peer[0:1, 0:1])).astype(BF)
 
     def written(i):
@@ -278,8 +326,8 @@
         out_specs=(hbm, hbm, whole),
         scratch_shapes=[
             vmem((SEQ, D), BF),
-            vmem((SEQ, GROUP * HS), BF),
-            vmem((SEQ, GROUP * HS), BF),
+            vmem((N_BLOCK, GROUP * BLOCK, HS), BF),
+            vmem((N_BLOCK, GROUP * BLOCK, HS), BF),
             vmem((D, HS), BF),
             vmem((D, HS), BF),
             vmem((SEQ, SEQ), F32),
@@ -291,16 +339,16 @@
             vmem((SEQ, HS), F32),
             vmem((SEQ, 2 * HS), BF),
             vmem((D, 2 * HS), F32),
-            vmem((8, 2 * HS), F32),
             vmem((D, 2 * HS), BF),
             vmem((D, 2 * HS), BF),
             vmem((D, HS), BF),
             vmem((D, HS), BF),
+            vmem((SEQ, SEQ), F32),
             vmem((8, 128), F32),
             vmem((3, 8, 128), F32),
             vmem((8, 128), F32),
             vmem((8, 128), F32),
-            dma((5,)),
+            dma((3,)),
             dma((N_IN,)),
             dma((N_IN,)),
             dma((N_IN,)),
@@ -313,6 +361,8 @@
             dma((N_OUT,)),
             dma,
             dma,
+            pltpu.SemaphoreType.REGULAR,
+            dma((2, GROUP)),
             dma((2, N_OUT)),
         ],
         compiler_params=pltpu.CompilerParams(
@@ -326,8 +376,9 @@
 
 def body(hidden_in, queries, out_grad, token_ids, key_weight, value_weight, push_weight, gossip):
     args = (
-        hidden_in[0], queries[0], out_grad[0], token_ids, key_weight[0], value_weight[0],
-        push_weight.reshape(1, 1),
+        hidden_in[0], queries.reshape(N_BLOCK, BLOCK, GROUP * HS),
+        out_grad.reshape(N_BLOCK, BLOCK, GROUP * HS), token_ids, key_weight[0],
+        value_weight[0], push_weight.reshape(1, 1),
     )
     new_key, new_value, new_push = lax.switch(
         gossip[0], [partial(run, level) for level in range(LEVELS)], *args

time: 178 us -> 172 us (0.966)
  Pallas kernels: 172 us -> 166 us
    pallas_call x1, Pallas kernels: 172 us -> 166 us  [run(): pl.pallas_call(partial(kernel, 1 << level), name=f'gossip_step_{1 << leve...]
where the time goes in v2:
time: 172 us
  Pallas kernels  166 us (97%)
  between operations  3.04 us (2%)
  local copies, waits for them, and re-layouts  2.64 us (2%)
    pallas_call x1, Pallas kernels, run(): pl.pallas_call(partial(kernel, 1 << level), name=f'gossip_step_{1 << leve...  166 us

profile of v2, /device:TPU:1, one launch (start us, length us, event | category | flops | bytes accessed | tf_op | source)
XLA Modules:
  0.0 171.8 jit_solution(14845749490681900914)
XLA Ops:
  1.3 166.1 %conditional.1 = ((bf16[8192,128]{1,0:T(8,128)(2,1)S(1)}, bf16[8192,128]{1,0:T(8,128)(2,1)S(1)}, bf16[1,1]{1,0:T(2,128)(2,1)})) conditional(s32[]{:T(128)} %bitcast, (bf16[128,8192]{1,0:T(8,128)(2,1)}, bf16[4,128,1024]{2,1,0:T(8,128)(2,1)}, bf16[4,128,1024]{2,1,0:T(8,128)(2,1)}, s32[1,512]{1,0:T(1,128)}, ...), branch_computations={%region_0.0_spmd, %region_1.0_spmd, %region_2.0_spmd} | conditional | flops 7000000000 | bytes 16777224 | solution.py:383
  1.3 165.8 %gossip_step_1.1 = (bf16[8192,128]{1,0:T(8,128)(2,1)S(1)}, bf16[8192,128]{1,0:T(8,128)(2,1)S(1)}, bf16[1,1]{1,0:T(2,128)(2,1)}) custom-call(bf16[128,8192]{1,0:T(8,128)(2,1)} %get-tuple-element.54.hid, bf16[4,128,1024]{2,1,0:T(8,128)(2,1)} %get-tuple-element.55.qin, bf16[4,128,1024]{2,1,0:T(8,128)(2,1)} %get-tuple-element.56.gin, ...), custom_call_target="tpu_custom_call" | custom-call | flops 7000000000 | bytes 16777216 | tf_op jit(solution)/shard_map/cond/branch_0_fun/gossip_step_1/pallas_call | solution.py:317
  167.4 1.3 copy.23
  168.7 1.3 copy.24

commit v3 on v2

--- a/solution.py
+++ b/solution.py
@@ -28,11 +28,11 @@
 
 COLS = 512
 N_IN = D // COLS
-ROWS = 256
+ROWS = 512
 N_OUT = D // ROWS
 BLOCK = 128
 N_BLOCK = SEQ // BLOCK
-SPAN = 1
+SPAN = 2
 WIDE = 1024
 
 
@@ -53,11 +53,11 @@
     hid, qin, gin, ids, kin, vin, push,
     out_k, out_v, out_push,
     hbuf, qbuf, gbuf, kw, vw, bias, zbuf, acc, krow, vrow, gk, gv, gpair, gw,
-    abuf, rbuf, ostk, ostv, gram,
-    sq_mine, sq_peer, push_mine, push_peer,
+    abuf, rbuf, ostk, ostv, gram, kw_peer, vw_peer, starts, seg_row,
+    sq_mine, sq_peer, push_mine, push_peer, factor_mine, factor_peer,
     load_sem, y2_send, y2_recv, fw_send, fw_recv, core_send, core_recv,
     sq_send, sq_recv, rep_send, rep_recv, push_send, push_recv,
-    credit, head_sem, out_sem,
+    factor_send, factor_recv, ahead_send, ahead_recv, credit, head_sem, out_sem,
 ):
     rep = lax.axis_index("rep")
     tp = lax.axis_index("tp")
@@ -128,15 +128,28 @@
         copy.start()
 
     with jax.named_scope("mask"):
-        down = lax.broadcasted_iota(jnp.int32, (SEQ, SEQ), 0)
-        over = lax.broadcasted_iota(jnp.int32, (SEQ, SEQ), 1)
-        starts = jnp.broadcast_to((ids[...] == doc_start).astype(F32), (8, SEQ)).astype(BF)
-        upper = (down <= over).astype(F32).astype(BF)
-        lower = (over <= down).astype(F32).astype(BF)
-        seg_row = dot_nn(starts, upper)
-        seg_col = dot_nt(lower, starts)
-        allowed = (down <= over) & (seg_col[:, 0:1] == seg_row[0:1, :])
-        bias[...] = jnp.where(allowed, 0.0, -1e30)
+        starts[...] = jnp.broadcast_to((ids[...] == doc_start).astype(F32), (16, SEQ)).astype(BF)
+        seg_row[...] = jnp.zeros_like(seg_row)
+        down = lax.broadcasted_iota(jnp.int32, (BLOCK, SEQ), 0)
+        over = lax.broadcasted_iota(jnp.int32, (BLOCK, SEQ), 1)
+
+        def add_row(n, carry):
+            first = pl.multiple_of(n * BLOCK, BLOCK)
+            upper = (down + first <= over).astype(F32).astype(BF)
+            seg_row[...] += dot_nn(starts[:, pl.ds(first, BLOCK)], upper)
+            return carry
+
+        lax.fori_loop(0, N_BLOCK, add_row, 0)
+
+        def mask_rows(n, carry):
+            first = pl.multiple_of(n * BLOCK, BLOCK)
+            lower = (over <= down + first).astype(F32).astype(BF)
+            seg_col = dot_nt(lower, starts[...])
+            allowed = (down + first <= over) & (seg_col[:, 0:1] == seg_row[0:1, :])
+            bias[pl.ds(first, BLOCK), :] = jnp.where(allowed, 0.0, -1e30)
+            return carry
+
+        lax.fori_loop(0, N_BLOCK, mask_rows, 0)
 
     acc[...] = jnp.zeros_like(acc)
     gk[...] = jnp.zeros_like(gk)
@@ -168,6 +181,13 @@
 
     with jax.named_scope("project"):
         lax.fori_loop(0, N_IN + 1, project, 0)
+
+    ahead = [
+        remote(src.at[pl.ds(0, ROWS)], dst, ahead_send.at[n], ahead_recv.at[n], target)
+        for n, (src, dst) in enumerate([(kin, kw_peer), (vin, vw_peer)])
+    ]
+    for copy in ahead:
+        copy.start()
 
     scale_model = 1.0 / math.sqrt(D)
     head_scale = 1.0 / math.sqrt(HS)
@@ -208,63 +228,74 @@
     gpair[:, 0:HS] = (gk[...] * head_scale).astype(BF)
     gpair[:, HS:] = gv[...].astype(BF)
 
-    with jax.named_scope("squares"):
-        pair = gpair[...]
-        high = gram[...].astype(BF)
-        rest = gram[...] - high.astype(F32)
-        middle = rest.astype(BF)
-        low = (rest - middle.astype(F32)).astype(BF)
-        spread = dot_nn(low, pair) + dot_nn(middle, pair) + dot_nn(high, pair)
-        total = jnp.sum(spread * pair.astype(F32), keepdims=True)
-        sq_mine[...] = jnp.broadcast_to(
-            jnp.maximum(total, 0.0) * (scale_model * scale_model), (8, 128)
-        )
+    def weight_grad(i):
+        rows = pl.ds(pl.multiple_of(i * ROWS, ROWS), ROWS)
+        gw[rows, :] = dot_tn(hbuf[:, rows], gpair[...]) * scale_model
+
+    def along(i):
+        rows = pl.ds(pl.multiple_of(i * ROWS, ROWS), ROWS)
+        return remote(abuf.at[rows], rbuf.at[rows], rep_send.at[i], rep_recv.at[i], target)
+
     shares = [
         remote(sq_mine, sq_peer.at[n], sq_send.at[n], sq_recv.at[n], device)
         for n, device in enumerate((other_core, other_half, diagonal))
     ]
-    for copy in shares:
-        copy.start()
-
-    def weight_grad(i):
-        rows = pl.ds(pl.multiple_of(i * ROWS, ROWS), ROWS)
-        gw[rows, :] = dot_tn(hbuf[:, rows], gpair[...]) * scale_model
-
-    weight_grad(0)
-    push_along.wait()
-    for copy in shares:
-        copy.wait()
-    squares = (sq_mine[0:1, 0:1] + sq_peer[0, 0:1, 0:1]) + (
-        sq_peer[1, 0:1, 0:1] + sq_peer[2, 0:1, 0:1]
-    )
-    factor = lax.rsqrt(squares / (2 * D * KVH * HS) + epsilon)
-    pl.semaphore_signal(credit, inc=1, device_id=source, device_id_type=MESH)
+    factor_along = remote(factor_mine, factor_peer, factor_send, factor_recv, target)
+
+    def share_squares():
+        def add_rows(n, total):
+            rows = pl.ds(pl.multiple_of(n * 256, 256), 256)
+            pair = gpair[...]
+            whole = gram[rows, :]
+            high = whole.astype(BF)
+            rest = whole - high.astype(F32)
+            middle = rest.astype(BF)
+            low = (rest - middle.astype(F32)).astype(BF)
+            spread = dot_nn(low, pair) + dot_nn(middle, pair) + dot_nn(high, pair)
+            return total + jnp.sum(spread * gpair[rows, :].astype(F32), axis=0, keepdims=True)
+
+        total = lax.fori_loop(0, SEQ // 256, add_rows, jnp.zeros((1, 2 * HS), F32))
+        total = jnp.maximum(jnp.sum(total, keepdims=True), 0.0) * (scale_model * scale_model)
+        sq_mine[...] = jnp.broadcast_to(total, (8, 128))
+        for copy in shares:
+            copy.start()
+
+    def settle_factor():
+        push_along.wait()
+        for copy in shares:
+            copy.wait()
+        squares = (sq_mine[...] + sq_peer[0]) + (sq_peer[1] + sq_peer[2])
+        factor_mine[...] = lax.rsqrt(squares / (2 * D * KVH * HS) + epsilon)
+        pl.semaphore_signal(credit, inc=1, device_id=source, device_id_type=MESH)
+        factor_along.start()
+        pl.semaphore_wait(credit, 1)
 
     def own_part(rows):
-        step = (gw[rows, :] * factor).astype(BF).astype(F32)
+        step = (gw[rows, :] * factor_mine[0:1, 0:1]).astype(BF).astype(F32)
         own_k = 0.5 * kw[rows, :].astype(F32) - (0.5 * learn_rate) * step[:, 0:HS]
         own_v = 0.5 * vw[rows, :].astype(F32) - (0.5 * learn_rate) * step[:, HS:]
         return own_k, own_v
 
-    def along(i):
-        rows = pl.ds(pl.multiple_of(i * ROWS, ROWS), ROWS)
-        return remote(abuf.at[rows], rbuf.at[rows], rep_send.at[i], rep_recv.at[i], target)
-
     def send_part(i, carry):
         rows = pl.ds(pl.multiple_of(i * ROWS, ROWS), ROWS)
-        own_k, own_v = own_part(rows)
-        abuf[rows, 0:HS] = own_k.astype(BF)
-        abuf[rows, HS:] = own_v.astype(BF)
+        weight_grad(i)
 
         @pl.when(i == 0)
         def _():
-            pl.semaphore_wait(credit, 1)
-
-        along(i).start()
-
-        @pl.when(i + 1 < N_OUT)
-        def _():
-            weight_grad(i + 1)
+            abuf[rows, :] = gw[rows, :].astype(BF)
+            along(i).start()
+            share_squares()
+
+        @pl.when(i == 1)
+        def _():
+            settle_factor()
+
+        @pl.when(i > 0)
+        def _():
+            own_k, own_v = own_part(rows)
+            abuf[rows, 0:HS] = own_k.astype(BF)
+            abuf[rows, HS:] = own_v.astype(BF)
+            along(i).start()
 
         return carry
 
@@ -284,12 +315,27 @@
         rows = pl.ds(pl.multiple_of(i * ROWS, ROWS), ROWS)
         own_k, own_v = own_part(rows)
         along(i).wait_recv()
-        ostk[rows, :] = (own_k + rbuf[rows, 0:HS].astype(F32)).astype(BF)
-        ostv[rows, :] = (own_v + rbuf[rows, HS:].astype(F32)).astype(BF)
+
+        @pl.when(i == 0)
+        def _():
+            step = (rbuf[rows, :].astype(F32) * factor_peer[0:1, 0:1]).astype(BF).astype(F32)
+            peer_k = 0.5 * kw_peer[...].astype(F32) - (0.5 * learn_rate) * step[:, 0:HS]
+            peer_v = 0.5 * vw_peer[...].astype(F32) - (0.5 * learn_rate) * step[:, HS:]
+            ostk[rows, :] = (own_k + peer_k).astype(BF)
+            ostv[rows, :] = (own_v + peer_v).astype(BF)
+
+        @pl.when(i > 0)
+        def _():
+            ostk[rows, :] = (own_k + rbuf[rows, 0:HS].astype(F32)).astype(BF)
+            ostv[rows, :] = (own_v + rbuf[rows, HS:].astype(F32)).astype(BF)
+
         for copy in written(i):
             copy.start()
         return carry
 
+    factor_along.wait()
+    for copy in ahead:
+        copy.wait()
     with jax.named_scope("mix"):
         lax.fori_loop(0, N_OUT, mix, 0)
 
@@ -344,8 +390,14 @@
             vmem((D, HS), BF),
             vmem((D, HS), BF),
             vmem((SEQ, SEQ), F32),
+            vmem((ROWS, HS), BF),
+            vmem((ROWS, HS), BF),
+            vmem((16, SEQ), BF),
+            vmem((16, SEQ), F32),
             vmem((8, 128), F32),
             vmem((3, 8, 128), F32),
+            vmem((8, 128), F32),
+            vmem((8, 128), F32),
             vmem((8, 128), F32),
             vmem((8, 128), F32),
             dma((3,)),
@@ -361,6 +413,10 @@
             dma((N_OUT,)),
             dma,
             dma,
+            dma,
+            dma,
+            dma((2,)),
+            dma((2,)),
             pltpu.SemaphoreType.REGULAR,
             dma((2, GROUP)),
             dma((2, N_OUT)),

time: 172 us -> 169 us (0.983)
  Pallas kernels: 166 us -> 163 us
    pallas_call x1, Pallas kernels: 166 us -> 163 us  [run(): pl.pallas_call(partial(kernel, 1 << level), name=f'gossip_step_{1 << leve...]
where the time goes in v3:
time: 169 us
  Pallas kernels  163 us (96%)
  between operations  3.04 us (2%)
  local copies, waits for them, and re-layouts  2.64 us (2%)
    pallas_call x1, Pallas kernels, run(): pl.pallas_call(partial(kernel, 1 << level), name=f'gossip_step_{1 << leve...  163 us

profile of v3, /device:TPU:1, one launch (start us, length us, event | category | flops | bytes accessed | tf_op | source)
XLA Modules:
  0.0 169.0 jit_solution(10231224239309784403)
XLA Ops:
  1.3 163.3 %conditional.1 = ((bf16[8192,128]{1,0:T(8,128)(2,1)S(1)}, bf16[8192,128]{1,0:T(8,128)(2,1)S(1)}, bf16[1,1]{1,0:T(2,128)(2,1)})) conditional(s32[]{:T(128)} %bitcast, (bf16[128,8192]{1,0:T(8,128)(2,1)}, bf16[4,128,1024]{2,1,0:T(8,128)(2,1)}, bf16[4,128,1024]{2,1,0:T(8,128)(2,1)}, s32[1,512]{1,0:T(1,128)}, ...), branch_computations={%region_0.0_spmd, %region_1.0_spmd, %region_2.0_spmd} | conditional | flops 7000000000 | bytes 16777224 | solution.py:439
  1.3 163.0 %gossip_step_1.1 = (bf16[8192,128]{1,0:T(8,128)(2,1)S(1)}, bf16[8192,128]{1,0:T(8,128)(2,1)S(1)}, bf16[1,1]{1,0:T(2,128)(2,1)}) custom-call(bf16[128,8192]{1,0:T(8,128)(2,1)} %get-tuple-element.54.hid, bf16[4,128,1024]{2,1,0:T(8,128)(2,1)} %get-tuple-element.55.qin, bf16[4,128,1024]{2,1,0:T(8,128)(2,1)} %get-tuple-element.56.gin, ...), custom_call_target="tpu_custom_call" | custom-call | flops 7000000000 | bytes 16777216 | tf_op jit(solution)/shard_map/cond/branch_0_fun/gossip_step_1/pallas_call | solution.py:363
  164.6 1.3 copy.23
  165.9 1.3 copy.24

commit v4 on v3

--- a/solution.py
+++ b/solution.py
@@ -26,12 +26,13 @@
 F32 = jnp.float32
 MIB = 1024 * 1024
 
-COLS = 512
+COLS = 256
 N_IN = D // COLS
 ROWS = 512
 N_OUT = D // ROWS
 BLOCK = 128
 N_BLOCK = SEQ // BLOCK
+HALF = SEQ // 2
 SPAN = 2
 WIDE = 1024
 
@@ -175,7 +176,9 @@
             zbuf[:, HS:] = (vw[rows, :].astype(F32) * inverse).astype(BF)
             part = hbuf[:, rows]
             acc[...] += dot_nn(part, zbuf[...])
-            gram[...] += dot_nt(part, part)
+            top, bottom = part[0:HALF, :], part[HALF:, :]
+            gram[0:HALF, 0:HALF] += dot_nt(top, top)
+            gram[HALF:, :] += dot_nt(bottom, part)
 
         return carry
 
@@ -244,9 +247,10 @@
 
     def share_squares():
         def add_rows(n, total):
-            rows = pl.ds(pl.multiple_of(n * 256, 256), 256)
+            rows = pl.ds(pl.multiple_of(n * HALF, HALF), HALF)
             pair = gpair[...]
-            whole = gram[rows, :]
+            column = lax.broadcasted_iota(jnp.int32, (HALF, SEQ), 1)
+            whole = gram[rows, :] * jnp.where(column < n * HALF, 2.0, 1.0)
             high = whole.astype(BF)
             rest = whole - high.astype(F32)
             middle = rest.astype(BF)
@@ -254,7 +258,7 @@
             spread = dot_nn(low, pair) + dot_nn(middle, pair) + dot_nn(high, pair)
             return total + jnp.sum(spread * gpair[rows, :].astype(F32), axis=0, keepdims=True)
 
-        total = lax.fori_loop(0, SEQ // 256, add_rows, jnp.zeros((1, 2 * HS), F32))
+        total = lax.fori_loop(0, SEQ // HALF, add_rows, jnp.zeros((1, 2 * HS), F32))
         total = jnp.maximum(jnp.sum(total, keepdims=True), 0.0) * (scale_model * scale_model)
         sq_mine[...] = jnp.broadcast_to(total, (8, 128))
         for copy in shares:

time: 169 us -> 168 us (level)
  Pallas kernels: 163 us -> 161 us
    pallas_call x1, Pallas kernels: 163 us -> 161 us  [run(): pl.pallas_call(partial(kernel, 1 << level), name=f'gossip_step_{1 << leve...]
where the time goes in v4:
time: 168 us; the launch traced here: 167 us
  Pallas kernels  161 us (96%)
  between operations  3.04 us (2%)
  local copies, waits for them, and re-layouts  2.64 us (2%)
    pallas_call x1, Pallas kernels, run(): pl.pallas_call(partial(kernel, 1 << level), name=f'gossip_step_{1 << leve...  161 us

profile of v4, /device:TPU:1, one launch (start us, length us, event | category | flops | bytes accessed | tf_op | source)
XLA Modules:
  0.0 167.0 jit_solution(15457045703592766281)
XLA Ops:
  1.3 161.3 %conditional.1 = ((bf16[8192,128]{1,0:T(8,128)(2,1)S(1)}, bf16[8192,128]{1,0:T(8,128)(2,1)S(1)}, bf16[1,1]{1,0:T(2,128)(2,1)})) conditional(s32[]{:T(128)} %bitcast, (bf16[128,8192]{1,0:T(8,128)(2,1)}, bf16[4,128,1024]{2,1,0:T(8,128)(2,1)}, bf16[4,128,1024]{2,1,0:T(8,128)(2,1)}, s32[1,512]{1,0:T(1,128)}, ...), branch_computations={%region_0.0_spmd, %region_1.0_spmd, %region_2.0_spmd} | conditional | flops 7000000000 | bytes 16777224 | solution.py:443
  1.5 160.9 %gossip_step_4.1 = (bf16[8192,128]{1,0:T(8,128)(2,1)S(1)}, bf16[8192,128]{1,0:T(8,128)(2,1)S(1)}, bf16[1,1]{1,0:T(2,128)(2,1)}) custom-call(bf16[128,8192]{1,0:T(8,128)(2,1)} %get-tuple-element.74.hid, bf16[4,128,1024]{2,1,0:T(8,128)(2,1)} %get-tuple-element.75.qin, bf16[4,128,1024]{2,1,0:T(8,128)(2,1)} %get-tuple-element.76.gin, ...), custom_call_target="tpu_custom_call" | custom-call | flops 7000000000 | bytes 16777216 | tf_op jit(solution)/shard_map/cond/branch_2_fun/gossip_step_4/pallas_call | solution.py:367
  162.6 1.3 copy.23
  163.9 1.3 copy.24
